TPU v7x, 32 devices: a whole 2x2x4 slice. The times are simulated.
32 devices in a mesh: rep: 8 (over z, x), shard: 4 (over y, core).
Axes of the slice: x: 2, y: 2, z: 4, core: 2. Of those that a mesh axis runs over, the one named last changes fastest.
Arguments:
- tokens: bfloat16 [16384, 768], P(('rep', 'shard')), may hold values from -6 to 6
- cotangent: bfloat16 [16384, 768], P(('rep', 'shard')), may hold values from -6 to 6
- lengths: int32 [32, 4], P(('rep', 'shard')), may hold values from 0 to 512, as said below
- routes: int32 [2, 16384, 1], P(None, ('rep', 'shard')), may hold values from 0 to 1; in each aligned block of 512 rows (0 to 511, 512 to 1023, ..., all dimensions but the last counted through in order) at most 288 rows name the same one
- buckets: int32 [1023], replicated, may hold values from 0 to 31, as said below
- w_qkv: bfloat16 [2, 3, 768, 768], P(None, None, 'shard'), may hold values from -0.21875 to 0.21875
- w_attn_out: bfloat16 [2, 768, 768], P(None, 'shard'), may hold values from -0.875 to 0.875
- gains: bfloat16 [2, 2, 768], P(None, None, 'shard'), may hold values from 0.5 to 1.5
- router: bfloat16 [2, 768, 2], P(None, 'shard'), may hold values from -0.15625 to 0.15625
- w_in: bfloat16 [2, 2, 768, 3072], P(None, None, 'shard'), may hold values from -0.21875 to 0.21875
- w_out: bfloat16 [2, 2, 3072, 768], P(None, None, 'shard'), may hold values from -0.21875 to 0.21875
- bias_table: bfloat16 [32, 12], P('shard'), may hold values from -4 to 4
Outputs:
- out_tokens: bfloat16 [16384, 768], P(('rep', 'shard'))
- grad_tokens: float32 [16384, 768], P(('rep', 'shard'))
- grad_w_qkv: float32 [2, 3, 768, 768], P(None, None, 'shard')
- grad_w_attn_out: float32 [2, 768, 768], P(None, 'shard')
- grad_gains: float32 [2, 2, 768], P(None, None, 'shard')
- grad_router: float32 [2, 768, 2], P(None, 'shard')
- grad_w_in: float32 [2, 2, 768, 3072], P(None, None, 'shard')
- grad_w_out: float32 [2, 2, 3072, 768], P(None, None, 'shard')
- grad_bias_table: float32 [32, 12], P('shard')
Inputs may be any that keep to these rules, and one draw needn't show every extreme that they name: Each device's lengths sum to at most 512; one device holds a single sequence of 512 rows. `routes`: in each layer the rows of one device name each expert at most 288 times. buckets[511 + r] is 0 for r = 0, never falls as |r| grows on either side, is below 16 for r <= 0 and 16 or more for r > 0.
All inputs are finite; a program needn't handle non-finite values.
Results may differ from a plain program's by a relative error of at most 0.029.
Values may be sent and summed in bfloat16 or wider, within the bound.
A program may use at most 320 MiB of HBM per device.

v0:
```python
import jax
import jax.numpy as jnp
from jax import lax
from jax.sharding import PartitionSpec as P

H = 12
DH = 64
NB = 32
CAP = 288


EPSILON = 1e-06
NEGATIVE = -1e30
HIGHEST = lax.Precision.HIGHEST
BLOCK_LIMIT = 512


def inverse_rms(hidden):
    return lax.rsqrt(jnp.mean(hidden * hidden, axis=1, keepdims=True) + EPSILON)


def norm_backward(hidden, scaling, gain_row, upstream):
    weighted = upstream * gain_row
    inner = jnp.sum(weighted * hidden, axis=1, keepdims=True)
    cubed = scaling * scaling * scaling / hidden.shape[1]
    delta_hidden = scaling * weighted - cubed * hidden * inner
    delta_gain = jnp.sum(upstream * hidden * scaling, axis=0)
    return (delta_hidden, delta_gain)


def skew_bias(rel_rows, row_count, key_count):
    heads = rel_rows.shape[0]
    span = key_count + row_count - 1
    window = rel_rows
    window = jnp.pad(window, ((0, 0), (0, 1)))
    tiled = jnp.broadcast_to(window[:, None, :], (heads, row_count, span + 1)).reshape(heads, -1)
    tiled = tiled[:, : row_count * span].reshape(heads, row_count, span)
    return tiled[:, :, row_count - 1 : row_count - 1 + key_count]


def diagonal_sums(delta_scores):
    heads, row_count, key_count = delta_scores.shape
    span = key_count + row_count - 1
    flipped = jnp.pad(delta_scores[:, ::-1, :], ((0, 0), (0, 0), (0, row_count)))
    flat = flipped.reshape(heads, -1)[:, : row_count * span].reshape(heads, row_count, span)
    return jnp.sum(flat, axis=1)


def block_scores(queries, keys, rel_rows, segment, row_count):
    key_count = keys.shape[0]
    scores = jnp.einsum(
        "qhd,khd->hqk", queries, keys, preferred_element_type=jnp.float32
    ) * keys.shape[2] ** (-0.5)
    scores = scores + skew_bias(rel_rows, row_count, key_count)
    same_doc = segment[:, None] == segment[None, :]
    return jnp.where(same_doc[None], scores, NEGATIVE)


def attend_forward(queries, keys, values, rel_rows, segment):
    total = queries.shape[0]
    block_rows = min(BLOCK_LIMIT, total)
    masked = block_scores(queries, keys, rel_rows, segment, block_rows)
    highest = jnp.max(masked, axis=2, keepdims=True)
    exponent = jnp.exp(masked - highest)
    row_total = jnp.sum(exponent, axis=2, keepdims=True)
    weights = (exponent / row_total).astype(jnp.bfloat16)
    outputs = jnp.einsum("hqk,khd->qhd", weights, values, preferred_element_type=jnp.float32)
    log_parts = highest + jnp.log(row_total)
    return (outputs, log_parts)


def attend_backward(queries, keys, values, rel_rows, segment, log_sums, upstream):
    total, heads, head_dim = queries.shape
    scaling = head_dim ** (-0.5)
    block_rows = min(BLOCK_LIMIT, total)
    span = total + block_rows - 1
    delta_rel = jnp.zeros((2 * total - 1, heads), jnp.float32)
    masked = block_scores(queries, keys, rel_rows, segment, block_rows)
    weights = jnp.exp(masked - log_sums)
    delta_weights = jnp.einsum("qhd,khd->hqk", upstream, values, preferred_element_type=jnp.float32)
    inner = jnp.sum(weights * delta_weights, axis=2, keepdims=True)
    delta_scores = (weights * (delta_weights - inner)).astype(jnp.bfloat16)
    query_parts = (
        jnp.einsum("hqk,khd->qhd", delta_scores, keys, preferred_element_type=jnp.float32) * scaling
    )
    delta_keys = (
        jnp.einsum("hqk,qhd->khd", delta_scores, queries, preferred_element_type=jnp.float32)
        * scaling
    )
    delta_values = jnp.einsum(
        "hqk,qhd->khd", weights.astype(jnp.bfloat16), upstream, preferred_element_type=jnp.float32
    )
    begin = total - block_rows
    delta_rel = delta_rel.at[begin : begin + span].add(
        diagonal_sums(delta_scores.astype(jnp.float32)).T
    )
    return (query_parts, delta_keys, delta_values, delta_rel)


def body(
    tokens,
    cotangent,
    lengths,
    routes,
    buckets,
    w_qkv,
    w_attn_out,
    gains,
    router,
    w_in,
    w_out,
    bias_table,
):
    row_count = tokens.shape[0]
    layer_count = w_qkv.shape[0]
    experts = w_in.shape[1]
    slot_count = experts * CAP
    width = tokens.shape[1]
    positions = jnp.arange(row_count, dtype=jnp.int32)
    bounds = jnp.cumsum(lengths[0])
    segment = jnp.sum((positions[:, None] >= bounds[None, :]).astype(jnp.int32), axis=1)
    live_mask = (positions < bounds[-1]).astype(jnp.float32)[:, None]
    bucket_hot = (buckets[:, None] == jnp.arange(NB, dtype=jnp.int32)[None, :]).astype(jnp.float32)

    def make_plan(layer):
        route = routes[layer, :, 0]
        route_hot = (route[:, None] == jnp.arange(experts, dtype=jnp.int32)[None, :]).astype(
            jnp.int32
        )
        earlier = jnp.cumsum(route_hot, axis=0) - route_hot
        slot_index = route * CAP + jnp.sum(earlier * route_hot, axis=1)
        return (slot_index, route_hot.astype(jnp.float32))

    def backward_layer(upstream, saved, attn_params, expert_params, plan):
        projection, out_weight, gain_weight, table = attn_params
        in_weight, outer_weight, route_weight = expert_params
        slot_index, route_hot = plan
        (
            hidden,
            scale_one,
            normed_one,
            heads_in,
            attended,
            log_sums,
            rel_rows,
            middle,
            scale_two,
            normed_two,
            softmax_w,
            gate,
            placed,
            upward,
            active,
            combined,
        ) = saved
        gain_rows = gain_weight.astype(jnp.float32)
        delta_gate = jnp.sum(upstream * combined, axis=1, keepdims=True)
        scaled_up = (gate * upstream).astype(jnp.bfloat16)
        delta_expert = (
            jnp.zeros((slot_count, width), jnp.bfloat16)
            .at[slot_index]
            .set(scaled_up)
            .reshape(experts, CAP, width)
        )
        grad_outer = jnp.einsum(
            "ecf,ecd->efd", active, delta_expert, preferred_element_type=jnp.float32
        )
        delta_active = jnp.einsum(
            "ecd,efd->ecf", delta_expert, outer_weight, preferred_element_type=jnp.float32
        )
        gelu_pull = jax.vjp(lambda value: jax.nn.gelu(value, approximate=True), upward)[1]
        delta_upward = gelu_pull(delta_active)[0].astype(jnp.bfloat16)
        grad_inner = jnp.einsum(
            "ecd,ecf->edf", placed, delta_upward, preferred_element_type=jnp.float32
        )
        delta_placed = jnp.einsum(
            "ecf,edf->ecd", delta_upward, in_weight, preferred_element_type=jnp.float32
        ).reshape(slot_count, width)
        delta_logits = (softmax_w * (route_hot - gate) * delta_gate).astype(jnp.bfloat16)
        grad_route = jnp.einsum(
            "td,te->de", normed_two, delta_logits, preferred_element_type=jnp.float32
        )
        delta_normed_two = jnp.take(delta_placed, slot_index, axis=0) + jnp.einsum(
            "te,de->td", delta_logits, route_weight, preferred_element_type=jnp.float32
        )
        delta_middle, gain_two = norm_backward(middle, scale_two, gain_rows[1], delta_normed_two)
        delta_middle = delta_middle + upstream
        delta_branch = delta_middle.astype(jnp.bfloat16)
        grad_attn_out = jnp.einsum(
            "td,te->de", attended, delta_branch, preferred_element_type=jnp.float32
        )
        delta_attended = (
            jnp.einsum("te,de->td", delta_branch, out_weight, preferred_element_type=jnp.float32)
            .astype(jnp.bfloat16)
            .reshape(row_count, H, DH)
        )
        delta_query, delta_keys, delta_values, delta_rel = attend_backward(
            heads_in[0], heads_in[1], heads_in[2], rel_rows, segment, log_sums, delta_attended
        )
        delta_parts = [
            part.astype(jnp.bfloat16).reshape(row_count, H * DH)
            for part in (delta_query, delta_keys, delta_values)
        ]
        grad_projection = jnp.stack(
            [
                jnp.einsum("td,te->de", normed_one, part, preferred_element_type=jnp.float32)
                for part in delta_parts
            ]
        )
        delta_normed_one = jnp.einsum(
            "te,de->td", delta_parts[0], projection[0], preferred_element_type=jnp.float32
        )
        delta_normed_one = delta_normed_one + jnp.einsum(
            "te,de->td", delta_parts[1], projection[1], preferred_element_type=jnp.float32
        )
        delta_normed_one = delta_normed_one + jnp.einsum(
            "te,de->td", delta_parts[2], projection[2], preferred_element_type=jnp.float32
        )
        delta_hidden, gain_one = norm_backward(hidden, scale_one, gain_rows[0], delta_normed_one)
        delta_hidden = delta_hidden + delta_middle
        grad_table = jnp.dot(bucket_hot.T, delta_rel, precision=HIGHEST)
        grad_gain = jnp.stack([gain_one, gain_two])
        return (
            delta_hidden,
            (grad_projection, grad_attn_out, grad_gain, grad_table),
            (grad_inner, grad_outer, grad_route),
        )

    plans = [make_plan(layer) for layer in range(layer_count)]
    hidden = tokens.astype(jnp.float32)
    saved_list = []
    held_list = []
    for layer in range(layer_count):
        attn_params = (
            lax.all_gather(w_qkv[layer], "shard", axis=1, tiled=True),
            lax.all_gather(w_attn_out[layer], "shard", axis=0, tiled=True),
            lax.all_gather(gains[layer], "shard", axis=1, tiled=True),
            lax.all_gather(bias_table, "shard", axis=0, tiled=True),
        )
        expert_params = (
            lax.all_gather(w_in[layer], "shard", axis=1, tiled=True),
            lax.all_gather(w_out[layer], "shard", axis=1, tiled=True),
            lax.all_gather(router[layer], "shard", axis=0, tiled=True),
        )
        forward_projection, forward_out_weight, forward_gain_weight, forward_table = attn_params
        forward_in_weight, forward_outer_weight, forward_route_weight = expert_params
        forward_slot_index, forward_route_hot = plans[layer]
        forward_gain_rows = forward_gain_weight.astype(jnp.float32)
        forward_rel_rows = jnp.dot(
            bucket_hot, forward_table.astype(jnp.float32), precision=HIGHEST
        ).T
        forward_scale_one = inverse_rms(hidden)
        forward_normed_one = (hidden * forward_scale_one * forward_gain_rows[0]).astype(
            jnp.bfloat16
        )
        forward_heads_in = [
            jnp.dot(
                forward_normed_one, forward_projection[index], preferred_element_type=jnp.float32
            )
            .astype(jnp.bfloat16)
            .reshape(row_count, H, DH)
            for index in range(3)
        ]
        forward_attended, forward_log_sums = attend_forward(
            forward_heads_in[0], forward_heads_in[1], forward_heads_in[2], forward_rel_rows, segment
        )
        forward_attended = forward_attended.astype(jnp.bfloat16).reshape(row_count, H * DH)
        forward_middle = hidden + jnp.dot(
            forward_attended, forward_out_weight, preferred_element_type=jnp.float32
        )
        forward_scale_two = inverse_rms(forward_middle)
        forward_normed_two = (forward_middle * forward_scale_two * forward_gain_rows[1]).astype(
            jnp.bfloat16
        )
        logits = jnp.dot(
            forward_normed_two, forward_route_weight, preferred_element_type=jnp.float32
        )
        shifted = jnp.exp(logits - jnp.max(logits, axis=1, keepdims=True))
        forward_softmax_w = shifted / jnp.sum(shifted, axis=1, keepdims=True)
        forward_gate = jnp.sum(forward_softmax_w * forward_route_hot, axis=1, keepdims=True)
        forward_placed = (
            jnp.zeros((slot_count, width), jnp.bfloat16)
            .at[forward_slot_index]
            .set(forward_normed_two)
            .reshape(experts, CAP, width)
        )
        forward_upward = jnp.einsum(
            "ecd,edf->ecf", forward_placed, forward_in_weight, preferred_element_type=jnp.float32
        )
        forward_active = jax.nn.gelu(forward_upward, approximate=True).astype(jnp.bfloat16)
        expert_out = jnp.einsum(
            "ecf,efd->ecd", forward_active, forward_outer_weight, preferred_element_type=jnp.float32
        ).astype(jnp.bfloat16)
        forward_combined = jnp.take(
            expert_out.reshape(slot_count, width), forward_slot_index, axis=0
        ).astype(jnp.float32)
        result = forward_middle + forward_gate * forward_combined
        forward_saved = (
            hidden,
            forward_scale_one,
            forward_normed_one,
            forward_heads_in,
            forward_attended,
            forward_log_sums,
            forward_rel_rows,
            forward_middle,
            forward_scale_two,
            forward_normed_two,
            forward_softmax_w,
            forward_gate,
            forward_placed,
            forward_upward,
            forward_active,
            forward_combined,
        )
        hidden = result
        saved = forward_saved
        saved_list.append(saved)
        held_list.append((attn_params, expert_params))
    out_tokens = hidden.astype(jnp.bfloat16)
    gradient = cotangent.astype(jnp.float32) * live_mask
    projection_grads = [None] * layer_count
    attn_out_grads = [None] * layer_count
    gain_grads = [None] * layer_count
    inner_grads = [None] * layer_count
    outer_grads = [None] * layer_count
    route_grads = [None] * layer_count
    table_sum = None
    for layer in reversed(range(layer_count)):
        attn_params = (
            lax.all_gather(w_qkv[layer], "shard", axis=1, tiled=True),
            lax.all_gather(w_attn_out[layer], "shard", axis=0, tiled=True),
            lax.all_gather(gains[layer], "shard", axis=1, tiled=True),
            lax.all_gather(bias_table, "shard", axis=0, tiled=True),
        )
        expert_params = (
            lax.all_gather(w_in[layer], "shard", axis=1, tiled=True),
            lax.all_gather(w_out[layer], "shard", axis=1, tiled=True),
            lax.all_gather(router[layer], "shard", axis=0, tiled=True),
        )
        gradient, attn_part, expert_part = backward_layer(
            gradient, saved_list[layer], attn_params, expert_params, plans[layer]
        )
        projection_share, attn_out_share, gain_share, table_share = (
            lax.psum_scatter(
                attn_part[0].astype(jnp.bfloat16), "shard", scatter_dimension=1, tiled=True
            ).astype(jnp.float32),
            lax.psum_scatter(
                attn_part[1].astype(jnp.bfloat16), "shard", scatter_dimension=0, tiled=True
            ).astype(jnp.float32),
            lax.psum_scatter(
                attn_part[2].astype(jnp.bfloat16), "shard", scatter_dimension=1, tiled=True
            ).astype(jnp.float32),
            lax.psum_scatter(
                attn_part[3].astype(jnp.bfloat16), "shard", scatter_dimension=0, tiled=True
            ).astype(jnp.float32),
        )
        inner_share, outer_share, route_share = (
            lax.psum_scatter(
                expert_part[0].astype(jnp.bfloat16), "shard", scatter_dimension=1, tiled=True
            ).astype(jnp.float32),
            lax.psum_scatter(
                expert_part[1].astype(jnp.bfloat16), "shard", scatter_dimension=1, tiled=True
            ).astype(jnp.float32),
            lax.psum_scatter(
                expert_part[2].astype(jnp.bfloat16), "shard", scatter_dimension=0, tiled=True
            ).astype(jnp.float32),
        )
        projection_grads[layer] = projection_share
        attn_out_grads[layer] = attn_out_share
        gain_grads[layer] = gain_share
        inner_grads[layer] = inner_share
        outer_grads[layer] = outer_share
        route_grads[layer] = route_share
        table_sum = table_share if table_sum is None else table_sum + table_share
    grad_projection = jnp.stack(projection_grads)
    grad_attn_out = jnp.stack(attn_out_grads)
    grad_gains = jnp.stack(gain_grads)
    grad_router = jnp.stack(route_grads)
    grad_inner = jnp.stack(inner_grads)
    grad_outer = jnp.stack(outer_grads)
    grad_projection, grad_attn_out, grad_gains, grad_router, grad_inner, grad_outer, table_sum = (
        lax.psum(grad_projection.astype(jnp.bfloat16), "rep").astype(jnp.float32),
        lax.psum(grad_attn_out.astype(jnp.bfloat16), "rep").astype(jnp.float32),
        lax.psum(grad_gains.astype(jnp.bfloat16), "rep").astype(jnp.float32),
        lax.psum(grad_router.astype(jnp.bfloat16), "rep").astype(jnp.float32),
        lax.psum(grad_inner.astype(jnp.bfloat16), "rep").astype(jnp.float32),
        lax.psum(grad_outer.astype(jnp.bfloat16), "rep").astype(jnp.float32),
        lax.psum(table_sum.astype(jnp.bfloat16), "rep").astype(jnp.float32),
    )
    return (
        out_tokens,
        gradient,
        grad_projection,
        grad_attn_out,
        grad_gains,
        grad_router,
        grad_inner,
        grad_outer,
        table_sum,
    )


def solution(mesh):
    placed = (
        P(("rep", "shard"), None),
        P(("rep", "shard"), None),
        P(("rep", "shard"), None),
        P(None, ("rep", "shard"), None),
        P(),
        P(None, None, "shard", None),
        P(None, "shard", None),
        P(None, None, "shard"),
        P(None, "shard", None),
        P(None, None, "shard", None),
        P(None, None, "shard", None),
        P("shard", None),
    )
    return jax.shard_map(
        body,
        mesh=mesh,
        in_specs=placed,
        out_specs=(
            P(("rep", "shard"), None),
            P(("rep", "shard"), None),
            P(None, None, "shard", None),
            P(None, "shard", None),
            P(None, None, "shard"),
            P(None, "shard", None),
            P(None, None, "shard", None),
            P(None, None, "shard", None),
            P("shard", None),
        ),
        check_vma=False,
    )
```

profile of v0, /device:TPU:0, one launch (start us, length us, event | category | flops | bytes accessed | tf_op | source)
XLA Modules:
  0.0 1502.8 jit_solution(9295138013222689944)
XLA Ops:
  23.8 10.4 all-gather
  45.8 11.9 broadcast_in_dim.42
  57.7 10.9 pad.49
  68.7 39.7 %copy.160 = f32[2,8,512,1024]{3,1,2,0:T(8,128)} copy(f32[2,8,512,1024]{3,2,1,0:T(8,128)S(1)} %bitcast.280) | data formatting | bytes 67108864
  108.4 22.8 %slice.211 = f32[12,523776]{1,0:T(8,128)} slice(f32[12,524288]{1,0:T(8,128)} %bitcast.283), slice={[0:12], [0:523776]} | slice | bytes 50282496 | tf_op jit(solution)/shard_map/slice | solution.py:37
  131.2 41.9 %reshape.410 = f32[12,512,1023]{2,1,0:T(8,128)} reshape(f32[12,523776]{1,0:T(8,128)} %slice.211) | data formatting | bytes 50282496 | tf_op jit(solution)/shard_map/reshape | solution.py:37
  173.2 13.5 slice.212
  186.6 12.7 copy.154
  203.9 7.1 all-gather.3
  211.5 10.4 all-gather.6
  269.7 8.8 fusion.18
  278.6 9.1 fusion.60
  299.8 6.9 fusion.160
  320.8 9.0 fusion.10
  329.8 55.5 %all-gather.35.cloned.1.call-done = bf16[1,2,3072,768]{3,2,1,0:T(8,128)(2,1)} async-done(((bf16[1,2,768,768]{3,2,1,0:T(8,128)(2,1)}), bf16[1,2,3072,768]{3,2,1,0:T(8,128)(2,1)}) %all-gather.35.cloned.1.call-update) | async-done | bytes 9437200 | tf_op jit(solution)/shard_map/all_gather | solution.py:242
  385.3 9.0 fusion.63
  401.2 9.9 fusion.33
  434.9 9.2 multiply_reduce_fusion.1
  444.1 7.3 multiply_convert_fusion.1
  470.8 9.8 fusion.26
  513.9 10.9 multiply_reduce_fusion
  526.0 6.9 multiply_convert_fusion
  542.2 9.5 convolution_convert_fusion.2
  552.9 9.6 convolution_convert_fusion.3
  563.7 13.1 convolution_convert_fusion
  578.0 13.9 convolution_convert_fusion.1
  613.6 78.9 %reduce-scatter.31.cloned.1.call-done = bf16[2,192,3072]{2,1,0:T(8,128)(2,1)} async-done(((bf16[2,768,3072]{2,1,0:T(8,128)(2,1)}), bf16[2,192,3072]{2,1,0:T(8,128)(2,1)}) %reduce-scatter.31.cloned.1.call-update) | async-done | bytes 2359312 | tf_op jit(solution)/shard_map/reduce_scatter | solution.py:359
  692.4 81.5 %reduce-scatter.29.cloned.1.call-done = bf16[2,192,3072]{2,1,0:T(8,128)(2,1)} async-done(((bf16[2,768,3072]{2,1,0:T(8,128)(2,1)}), bf16[2,192,3072]{2,1,0:T(8,128)(2,1)}) %reduce-scatter.29.cloned.1.call-update) | async-done | bytes 2359312 | tf_op jit(solution)/shard_map/reduce_scatter | solution.py:359
  778.9 75.9 %reduce-scatter.35.cloned.1.call-done = bf16[2,768,768]{2,1,0:T(8,128)(2,1)} async-done(((bf16[2,3072,768]{2,1,0:T(8,128)(2,1)}), bf16[2,768,768]{2,1,0:T(8,128)(2,1)}) %reduce-scatter.35.cloned.1.call-update) | async-done | bytes 2359312 | tf_op jit(solution)/shard_map/reduce_scatter | solution.py:362
  854.9 80.9 %reduce-scatter.33.cloned.1.call-done = bf16[2,768,768]{2,1,0:T(8,128)(2,1)} async-done(((bf16[2,3072,768]{2,1,0:T(8,128)(2,1)}), bf16[2,768,768]{2,1,0:T(8,128)(2,1)}) %reduce-scatter.33.cloned.1.call-update) | async-done | bytes 2359312 | tf_op jit(solution)/shard_map/reduce_scatter | solution.py:362
  942.7 95.2 %rev.7 = f32[12,512,512]{1,2,0:T(8,128)} reverse(bf16[12,512,512]{1,2,0:T(8,128)(2,1)} %copy-done.3), dimensions={1} | reverse | bytes 18874368 | tf_op jit(solution)/shard_map/rev | solution.py:44
  1037.9 95.1 %rev.6 = f32[12,512,512]{1,2,0:T(8,128)} reverse(bf16[12,512,512]{1,2,0:T(8,128)(2,1)} %copy-done.2), dimensions={1} | reverse | bytes 18874368 | tf_op jit(solution)/shard_map/rev | solution.py:44
  1133.1 12.7 copy.159
  1145.7 14.5 pad.22.clone
  1160.3 11.0 pad.51
  1171.3 39.7 %copy.164 = f32[2,8,512,1024]{3,1,2,0:T(8,128)} copy(f32[2,8,512,1024]{3,2,1,0:T(8,128)S(1)} %bitcast.281) | data formatting | bytes 67108864
  1211.0 23.3 %slice.222 = f32[12,523776]{1,0:T(8,128)} slice(f32[12,524288]{1,0:T(8,128)} %bitcast.284), slice={[0:12], [0:523776]} | slice | bytes 50282496 | tf_op jit(solution)/shard_map/slice | solution.py:45
  1234.3 43.5 %reshape.437 = f32[12,512,1023]{2,1,0:T(8,128)} reshape(f32[12,523776]{1,0:T(8,128)} %slice.222) | data formatting | bytes 50282496 | tf_op jit(solution)/shard_map/reshape | solution.py:45
  1277.8 9.1 reduce_sum.275
  1286.9 12.7 copy.158
  1299.6 14.5 pad.21.clone
  1314.1 11.6 pad.50
  1325.7 39.7 %copy.163 = f32[2,8,512,1024]{3,1,2,0:T(8,128)} copy(f32[2,8,512,1024]{3,2,1,0:T(8,128)S(1)} %bitcast.282) | data formatting | bytes 67108864
  1365.4 22.7 %slice.221 = f32[12,523776]{1,0:T(8,128)} slice(f32[12,524288]{1,0:T(8,128)} %bitcast.285), slice={[0:12], [0:523776]} | slice | bytes 50282496 | tf_op jit(solution)/shard_map/slice | solution.py:45
  1388.1 41.6 %reshape.435 = f32[12,512,1023]{2,1,0:T(8,128)} reshape(f32[12,523776]{1,0:T(8,128)} %slice.221) | data formatting | bytes 50282496 | tf_op jit(solution)/shard_map/reshape | solution.py:45
  1429.8 9.6 reduce_sum.274
  1440.6 10.2 all-reduce.7
  1457.4 22.0 %all-reduce.5 = (bf16[2,2,192]{2,1,0:T(2,128)(2,1)S(1)}, bf16[2,192,2]{1,2,0:T(2,128)(2,1)S(1)}, bf16[8,12]{1,0:T(8,128)(2,1)S(1)}) all-reduce(bf16[2,2,192]{2,1,0:T(2,128)(2,1)S(1)} %pad_maximum_fusion.8, bf16[2,192,2]{1,2,0:T(2,128)(2,1)S(1)} %pad_maximum_fusion.9, ...), channel_id=1, replica_groups=mesh['rep'=8,'shard'=4] {'rep'}, use_global_device_ids=true, to_apply=%region_46.49 | all-reduce | flops 1632 | bytes 6528 | tf_op jit(solution)/shard_map/psum | solution.py:385
  (450 shorter events, 259.7 us)
Async XLA Ops:
  7.2 230.5 %all-gather.21.cloned.1.call-start = ((), (), s32[]{:S(2)}) async-start(), calls=%async_computation.20 | async-start | bytes 4423680 | tf_op jit(solution)/shard_map/all_gather | solution.py:235
  10.1 251.1 %all-gather.23.cloned.1.call-start = ((), (), s32[]{:S(2)}) async-start(), calls=%async_computation.21 | async-start | bytes 1474560 | tf_op jit(solution)/shard_map/all_gather | solution.py:236
  11.0 258.7 %all-gather.25.cloned.1.call-start = ((), (), s32[]{:S(2)}) async-start(), calls=%async_computation.22 | async-start | bytes 11796480 | tf_op jit(solution)/shard_map/all_gather | solution.py:241
  16.0 262.6 %all-gather.27.cloned.1.call-start = ((), (), s32[]{:S(2)}) async-start(), calls=%async_computation.23 | async-start | bytes 11796480 | tf_op jit(solution)/shard_map/all_gather | solution.py:242
  20.9 270.7 %all-gather.29.cloned.1.call-start = ((), (), s32[]{:S(2)}) async-start(), calls=%async_computation.24 | async-start | bytes 4423680 | tf_op jit(solution)/shard_map/all_gather | solution.py:235
  21.5 293.0 %all-gather.31.cloned.1.call-start = ((), (), s32[]{:S(2)}) async-start(), calls=%async_computation.25 | async-start | bytes 1474560 | tf_op jit(solution)/shard_map/all_gather | solution.py:236
  21.6 17.7 %copy-start.21 = (bf16[512,768]{1,0:T(8,128)(2,1)S(1)}, bf16[512,768]{1,0:T(8,128)(2,1)}, u32[]{:S(2)}) copy-start(bf16[512,768]{1,0:T(8,128)(2,1)} %param.24) | copy-start | bytes 2359300
  22.1 298.7 %all-gather.33.cloned.1.call-start = ((), (), s32[]{:S(2)}) async-start(), calls=%async_computation.26 | async-start | bytes 11796480 | tf_op jit(solution)/shard_map/all_gather | solution.py:241
  22.1 18.0 %copy-start.98 = (bf16[8,12]{1,0:T(8,128)(2,1)S(1)}, bf16[8,12]{1,0:T(8,128)(2,1)}, u32[]{:S(2)}) copy-start(bf16[8,12]{1,0:T(8,128)(2,1)} %param.35) | copy-start | bytes 580
  22.2 23.3 %copy-start.102 = (s32[1023]{0:T(1024)S(1)}, s32[1023]{0:T(1024)}, u32[]{:S(2)}) copy-start(s32[1023]{0:T(1024)} %param.28) | copy-start | bytes 12280
  22.8 362.4 %all-gather.35.cloned.1.call-start = ((), (), s32[]{:S(2)}) async-start(), calls=%async_computation.27 | async-start | bytes 11796480 | tf_op jit(solution)/shard_map/all_gather | solution.py:242
  23.6 581.8 %reduce-scatter.27.cloned.1.call-start = ((), (), s32[]{:S(2)}) async-start(), calls=%async_computation.15 | async-start | bytes 1474560 | tf_op jit(solution)/shard_map/reduce_scatter | solution.py:348
  39.2 203.5 %copy-start.71 = (f32[768]{0:T(1024)}, f32[768]{0:T(1024)S(1)}, u32[]{:S(2)}) copy-start(f32[768]{0:T(1024)S(1)} %get-tuple-element.62) | copy-start | bytes 9220
  39.3 228.2 %copy-start.65 = (f32[768]{0:T(1024)}, f32[768]{0:T(1024)S(1)}, u32[]{:S(2)}) copy-start(f32[768]{0:T(1024)S(1)} %get-tuple-element.61) | copy-start | bytes 9220
  40.1 202.7 %copy-start.80 = (f32[512]{0:T(512)}, f32[512]{0:T(512)S(1)}, u32[]{:S(2)}) copy-start(f32[512]{0:T(512)S(1)} %get-tuple-element.99) | copy-start | bytes 6148
  186.6 12.7 copy-start.104
  186.6 13.8 copy-start.85
  186.6 17.1 %copy-start.100 = (bf16[2,192,2]{1,2,0:T(2,128)(2,1)S(1)}, bf16[2,192,2]{1,2,0:T(2,128)(2,1)}, u32[]{:S(2)}) copy-start(bf16[2,192,2]{1,2,0:T(2,128)(2,1)} %param.32) | copy-start | bytes 4612
  200.4 68.6 %copy-start.67 = (s32[1,512,1]{1,2,0:T(1,128)}, s32[1,512,1]{1,2,0:T(1,128)S(1)}, u32[]{:S(2)}) copy-start(s32[1,512,1]{1,2,0:T(1,128)S(1)} %get-tuple-element.97) | copy-start | bytes 6148
  211.3 56.3 %copy-start.77 = (bf16[1,768,2]{1,2,0:T(2,128)(2,1)}, bf16[1,768,2]{1,2,0:T(2,128)(2,1)S(1)}, u32[]{:S(2)}) copy-start(bf16[1,768,2]{1,2,0:T(2,128)(2,1)S(1)} %copy.119) | copy-start | bytes 9220
  237.7 26.8 %copy-start.101 = (s32[512,1]{0,1:T(1,128)}, s32[512,1]{0,1:T(1,128)S(1)}, u32[]{:S(2)}) copy-start(s32[512,1]{0,1:T(1,128)S(1)} %get-tuple-element.95) | copy-start | bytes 6148
  240.1 15.9 %copy-start.38 = (bf16[512,768]{0,1:T(8,128)(2,1)}, bf16[512,768]{0,1:T(8,128)(2,1)S(1)}, u32[]{:S(2)}) copy-start(bf16[512,768]{0,1:T(8,128)(2,1)S(1)} %copy.113) | copy-start | bytes 2359300
  263.8 25.9 %copy-start.4 = (f32[512,768]{1,0:T(8,128)}, f32[512,768]{1,0:T(8,128)S(1)}, u32[]{:S(2)}) copy-start(f32[512,768]{1,0:T(8,128)S(1)} %get-tuple-element.113) | copy-start | bytes 4718596
  264.4 14.1 copy-start.69
  294.3 14.3 copy-start.40
  329.8 64.5 %copy-start.89 = (s32[1024]{0:T(1024)S(1)}, s32[1024]{0:T(1024)}, u32[]{:S(2)}) copy-start(s32[1024]{0:T(1024)} %pad_clamp_fusion) | copy-start | bytes 12292
  428.1 16.0 %slice-start.3 = ((s8[12582912]{0:T(1024)(128)(4,1)}), s8[4194304]{0:T(1024)(128)(4,1)S(1)}, s32[]{:S(2)}) async-start(s8[12582912]{0:T(1024)(128)(4,1)} %bitcast.278), calls=%async_computation.36 | async-start | bytes 8388608
  428.1 16.0 %slice-start.4 = ((s8[12582912]{0:T(1024)(128)(4,1)}), s8[4194304]{0:T(1024)(128)(4,1)S(1)}, s32[]{:S(2)}) async-start(s8[12582912]{0:T(1024)(128)(4,1)} %bitcast.278), calls=%async_computation.37 | async-start | bytes 8388608
  434.9 28.3 %copy-start.43 = (bf16[12,64,512]{2,1,0:T(8,128)(2,1)}, bf16[12,64,512]{2,1,0:T(8,128)(2,1)S(1)}, u32[]{:S(2)}) copy-start(bf16[12,64,512]{2,1,0:T(8,128)(2,1)S(1)} %fusion.75) | copy-start | bytes 2359300
  469.9 135.6 %reduce-scatter.25.cloned.1.call-start = ((), (), s32[]{:S(2)}) async-start(), calls=%async_computation.14 | async-start | bytes 1474560 | tf_op jit(solution)/shard_map/reduce_scatter | solution.py:348
  495.6 111.9 %reduce-scatter.23.cloned.1.call-start = ((), (), s32[]{:S(2)}) async-start(), calls=%async_computation.13 | async-start | bytes 4423680 | tf_op jit(solution)/shard_map/reduce_scatter | solution.py:345
  502.8 108.0 %reduce-scatter.21.cloned.1.call-start = ((), (), s32[]{:S(2)}) async-start(), calls=%async_computation.12 | async-start | bytes 4423680 | tf_op jit(solution)/shard_map/reduce_scatter | solution.py:345
  513.9 12.1 slice-start.2
  541.0 151.4 %reduce-scatter.31.cloned.1.call-start = ((), (), s32[]{:S(2)}) async-start(), calls=%async_computation.17 | async-start | bytes 11796480 | tf_op jit(solution)/shard_map/reduce_scatter | solution.py:359
  551.7 222.2 %reduce-scatter.29.cloned.1.call-start = ((), (), s32[]{:S(2)}) async-start(), calls=%async_computation.16 | async-start | bytes 11796480 | tf_op jit(solution)/shard_map/reduce_scatter | solution.py:359
  562.5 292.4 %reduce-scatter.35.cloned.1.call-start = ((), (), s32[]{:S(2)}) async-start(), calls=%async_computation.19 | async-start | bytes 11796480 | tf_op jit(solution)/shard_map/reduce_scatter | solution.py:362
  576.8 359.0 %reduce-scatter.33.cloned.1.call-start = ((), (), s32[]{:S(2)}) async-start(), calls=%async_computation.18 | async-start | bytes 11796480 | tf_op jit(solution)/shard_map/reduce_scatter | solution.py:362
  592.0 861.8 %reduce-scatter.39.cloned.1.call-start = ((), (), s32[]{:S(2)}) async-start(), calls=%async_computation.29 | async-start | bytes 245760
  602.1 852.5 %reduce-scatter.37.cloned.1.call-start = ((), (), s32[]{:S(2)}) async-start(), calls=%async_computation.28 | async-start | bytes 245760
  603.1 852.5 %reduce-scatter.43.cloned.1.call-start = ((), (), s32[]{:S(2)}) async-start(), calls=%async_computation.31 | async-start | bytes 245760
  604.2 852.2 %reduce-scatter.41.cloned.1.call-start = ((), (), s32[]{:S(2)}) async-start(), calls=%async_computation.30 | async-start | bytes 245760
  605.4 875.8 %all-reduce.10.cloned.1.call-start = ((), (), s32[]{:S(2)}) async-start(), calls=%async_computation.32 | async-start | bytes 23592960 | tf_op jit(solution)/shard_map/psum | solution.py:383
  1429.7 21.0 %copy-start.10 = (f32[512,768]{1,0:T(8,128)S(1)}, f32[512,768]{1,0:T(8,128)}, u32[]{:S(2)}) copy-start(f32[512,768]{1,0:T(8,128)} %copy-done.9) | copy-start | bytes 4718596
  1429.7 21.0 %copy-start.23 = (bf16[512,768]{1,0:T(8,128)(2,1)S(1)}, bf16[512,768]{1,0:T(8,128)(2,1)}, u32[]{:S(2)}) copy-start(bf16[512,768]{1,0:T(8,128)(2,1)} %param.24) | copy-start | bytes 2359300
  1429.7 21.0 %copy-start.73 = (f32[768]{0:T(1024)S(1)}, f32[768]{0:T(1024)}, u32[]{:S(2)}) copy-start(f32[768]{0:T(1024)} %copy-done.71) | copy-start | bytes 9220
  1429.7 21.0 %copy-start.82 = (f32[512]{0:T(512)S(1)}, f32[512]{0:T(512)}, u32[]{:S(2)}) copy-start(f32[512]{0:T(512)} %copy-done.80) | copy-start | bytes 6148
  1429.8 21.0 %copy-start.90 = (f32[512]{0:T(512)S(1)}, f32[512]{0:T(512)}, u32[]{:S(2)}) copy-start(f32[512]{0:T(512)} %get-tuple-element.58) | copy-start | bytes 6148
  1429.8 21.0 %copy-start.91 = (f32[512]{0:T(512)S(1)}, f32[512]{0:T(512)}, u32[]{:S(2)}) copy-start(f32[512]{0:T(512)} %get-tuple-element.98) | copy-start | bytes 6148
  (89 other events, 386.1 us)
Sparse Core Ops, SparseCore 0:
  10.2 35.5 all-gather.20
  47.4 17.4 all-gather.22
  66.4 64.2 all-gather.24
  132.7 64.2 all-gather.26
  198.9 33.2 all-gather.28
  233.6 18.7 all-gather.30
  254.6 64.2 all-gather.32
  321.0 64.2 all-gather.34
  470.0 25.7 reduce-scatter.26
  498.4 25.6 reduce-scatter.24
  527.2 40.4 reduce-scatter.22
  570.3 40.4 reduce-scatter.20
  614.0 78.4 reduce-scatter.30
  695.5 78.4 reduce-scatter.28
  776.4 78.4 reduce-scatter.34
  857.3 78.4 reduce-scatter.32
  938.1 19.7 reduce-scatter.38
  960.2 19.7 reduce-scatter.36
  982.5 19.8 reduce-scatter.42
  1004.6 19.7 reduce-scatter.40
  1029.7 364.5 all-reduce.9
where the time goes:
time: 1530 us; the launch traced here: 1500 us
  local copies, waits for them, and re-layouts  697 us (46%)
  waiting for transfers between devices  379 us (25%)
  matrix products  233 us (15%)
  other arithmetic  103 us (7%)
  blocking collectives  72.1 us (5%)
  between operations  17.2 us (1%)
    unnamed x254, local copies, waits for them, and re-layouts  218 us
    rev x2, local copies, waits for them, and re-layouts, diagonal_sums(): delta_scores[:, ::-1, :]  190 us
    reduce_scatter x2, waiting for transfers between devices, body(): lax.psum_scatter(expert_part[0].astype(jnp.bfloat16), 'shard', scatter_di...  160 us
    reduce_scatter x2, waiting for transfers between devices, body(): lax.psum_scatter(expert_part[1].astype(jnp.bfloat16), 'shard', scatter_di...  157 us
    reshape x2, local copies, waits for them, and re-layouts, diagonal_sums(): flipped.reshape(heads, -1)[:, :row_count * span]  85.1 us
    all_gather x2, waiting for transfers between devices, body(): lax.all_gather(w_out[layer], 'shard', axis=1, tiled=True)  55.5 us
    slice x2, local copies, waits for them, and re-layouts, diagonal_sums(): flipped.reshape(heads, -1)[:, :row_count * span]  46 us
    reshape x1, local copies, waits for them, and re-layouts, skew_bias(): tiled = tiled[:, :row_count * span].reshape(heads, row_count, span)  41.9 us
  transfers between devices with their start and end apart: 21, of which 6 were waited for; matrix products, arithmetic and copies ran while one was open for 61% of the time, Pallas kernels for 0%

commit v1 on v0

v1 whole, which is shorter than its diff:
```python
import functools

import jax
import jax.numpy as jnp
from jax import lax
from jax.experimental import pallas as pl
from jax.experimental.pallas import tpu as pltpu
from jax.sharding import PartitionSpec as P

H = 12
DH = 64
NB = 32
CAP = 288
PAIR = 2 * DH
STRIP = 128

EPSILON = 1e-06
NEGATIVE = -1e30
HIGHEST = lax.Precision.HIGHEST
F32 = jnp.float32
BF16 = jnp.bfloat16


def matmul(a, b, dims=((1,), (0,))):
    return lax.dot_general(a, b, (dims, ((), ())), preferred_element_type=F32)


def inverse_rms(hidden):
    return lax.rsqrt(jnp.mean(hidden * hidden, axis=1, keepdims=True) + EPSILON)


def norm_backward(hidden, scaling, gain_row, upstream):
    weighted = upstream * gain_row
    inner = jnp.sum(weighted * hidden, axis=1, keepdims=True)
    cubed = scaling * scaling * scaling / hidden.shape[1]
    delta_hidden = scaling * weighted - cubed * hidden * inner
    delta_gain = jnp.sum(upstream * hidden * scaling, axis=0)
    return (delta_hidden, delta_gain)


def strip_bias(rel_row, total):
    span = 2 * total
    wide = jnp.broadcast_to(rel_row, (STRIP, span))
    strip = pltpu.roll(wide, span - (STRIP - 1), 1, stride=1, stride_axis=0)
    first = total - STRIP
    return jnp.concatenate(
        [strip[:, first - begin : first - begin + total] for begin in range(0, total, STRIP)],
        axis=0,
    )


def strip_sums(delta_scores, mirror, total):
    span = 2 * total
    first = total - STRIP
    acc = jnp.zeros((STRIP, span), F32)
    for begin in range(0, total, STRIP):
        part = matmul(mirror, delta_scores[begin : begin + STRIP])
        left = first - begin
        pieces = [part, jnp.zeros((STRIP, span - total - left), F32)]
        if left:
            pieces = [jnp.zeros((STRIP, left), F32)] + pieces
        acc = acc + jnp.concatenate(pieces, axis=1)
    skewed = pltpu.roll(acc, 0, 1, stride=1, stride_axis=0)
    return jnp.sum(skewed, axis=0, keepdims=True)


def head_weights(queries, keys, rel_row, same, total):
    scores = matmul(queries, keys, ((1,), (1,))) * DH ** (-0.5) + strip_bias(rel_row, total)
    scores = jnp.where(same, scores, NEGATIVE)
    exponent = jnp.exp(scores - jnp.max(scores, axis=1, keepdims=True))
    return exponent * (1.0 / jnp.sum(exponent, axis=1, keepdims=True))


def forward_kernel(rel_ref, row_seg_ref, col_seg_ref, q_ref, k_ref, v_ref, o_ref):
    total = q_ref.shape[0]
    same = row_seg_ref[...] == col_seg_ref[...]
    low_half = lax.broadcasted_iota(jnp.int32, (total, PAIR), 1) < DH
    q, k, v = q_ref[...], k_ref[...], v_ref[...]
    zero = jnp.zeros_like(q)
    outs = []
    for side in range(2):
        mine = low_half if side == 0 else jnp.logical_not(low_half)
        weights = head_weights(
            jnp.where(mine, q, zero), k, rel_ref[side : side + 1, :], same, total
        )
        outs.append(matmul(weights.astype(BF16), v))
    o_ref[...] = jnp.where(low_half, outs[0], outs[1]).astype(BF16)


def backward_kernel(
    rel_ref, row_seg_ref, col_seg_ref, q_ref, k_ref, v_ref, do_ref, dqkv_ref, drel_ref
):
    total = q_ref.shape[0]
    same = row_seg_ref[...] == col_seg_ref[...]
    low_half = lax.broadcasted_iota(jnp.int32, (total, PAIR), 1) < DH
    mirror = (
        lax.broadcasted_iota(jnp.int32, (STRIP, STRIP), 0)
        + lax.broadcasted_iota(jnp.int32, (STRIP, STRIP), 1)
        == STRIP - 1
    ).astype(F32).astype(BF16)
    q, k, v, do = q_ref[...], k_ref[...], v_ref[...], do_ref[...]
    zero = jnp.zeros_like(q)
    scaling = DH ** (-0.5)
    outs = []
    for side in range(2):
        mine = low_half if side == 0 else jnp.logical_not(low_half)
        weights = head_weights(
            jnp.where(mine, q, zero), k, rel_ref[side : side + 1, :], same, total
        )
        delta_weights = matmul(jnp.where(mine, do, zero), v, ((1,), (1,)))
        inner = jnp.sum(weights * delta_weights, axis=1, keepdims=True)
        delta_scores = (weights * (delta_weights - inner)).astype(BF16)
        outs.append(
            (
                matmul(delta_scores, k) * scaling,
                matmul(delta_scores, q, ((0,), (0,))) * scaling,
                matmul(weights.astype(BF16), do, ((0,), (0,))),
            )
        )
        drel_ref[side : side + 1, :] = strip_sums(delta_scores, mirror, total)
    for index in range(3):
        dqkv_ref[index] = jnp.where(low_half, outs[0][index], outs[1][index]).astype(BF16)


def attention_specs(total):
    rel = pl.BlockSpec((None, 2, 2 * total), lambda i: (i, 0, 0))
    row_seg = pl.BlockSpec((total, 1), lambda i: (0, 0))
    col_seg = pl.BlockSpec((1, total), lambda i: (0, 0))
    qkv = [
        pl.BlockSpec((None, total, PAIR), functools.partial(lambda which, i: (which, 0, i), which))
        for which in range(3)
    ]
    return [rel, row_seg, col_seg] + qkv


def attend_forward(rel_pairs, row_seg, col_seg, qkv):
    total, width = qkv.shape[1:]
    return pl.pallas_call(
        forward_kernel,
        grid=(H // 2,),
        in_specs=attention_specs(total),
        out_specs=pl.BlockSpec((total, PAIR), lambda i: (0, i)),
        out_shape=jax.ShapeDtypeStruct((total, width), BF16),
        compiler_params=pltpu.CompilerParams(vmem_limit_bytes=40 * 2**20),
        cost_estimate=pl.CostEstimate(
            flops=4 * H * total * total * DH * 4, bytes_accessed=8 * total * width,
            transcendentals=H * total * total,
        ),
        name="attend_forward",
    )(rel_pairs, row_seg, col_seg, qkv, qkv, qkv)


def attend_backward(rel_pairs, row_seg, col_seg, qkv, upstream):
    total, width = qkv.shape[1:]
    return pl.pallas_call(
        backward_kernel,
        grid=(H // 2,),
        in_specs=attention_specs(total) + [pl.BlockSpec((total, PAIR), lambda i: (0, i))],
        out_specs=[
            pl.BlockSpec((3, total, PAIR), lambda i: (0, 0, i)),
            pl.BlockSpec((None, 2, 2 * total), lambda i: (i, 0, 0)),
        ],
        out_shape=[
            jax.ShapeDtypeStruct((3, total, width), BF16),
            jax.ShapeDtypeStruct((H // 2, 2, 2 * total), F32),
        ],
        compiler_params=pltpu.CompilerParams(vmem_limit_bytes=40 * 2**20),
        cost_estimate=pl.CostEstimate(
            flops=10 * H * total * total * DH * 4, bytes_accessed=16 * total * width,
            transcendentals=H * total * total,
        ),
        name="attend_backward",
    )(rel_pairs, row_seg, col_seg, qkv, qkv, qkv, upstream)


def exchange(blocks_for, place, count, start):
    me = lax.axis_index("shard")
    held = place(start, blocks_for(me), me)
    for step in range(1, count):
        towards = lax.rem(me + step, count)
        source = lax.rem(me + count - step, count)
        pairs = [(i, (i + step) % count) for i in range(count)]
        got = lax.ppermute(blocks_for(towards), "shard", pairs)
        held = place(held, got, source)
    return held


def columns_from_rows(weight, count):
    experts, rows, cols = weight.shape
    part = cols // count

    def block(target):
        return lax.dynamic_slice(weight, (0, 0, target * part), (experts, rows, part))

    def place(held, got, source):
        return lax.dynamic_update_slice(held, got, (0, source * rows, 0))

    return exchange(block, place, count, jnp.zeros((experts, rows * count, part), weight.dtype))


def rows_from_columns(weight, count):
    experts, rows, cols = weight.shape
    part = rows // count

    def block(target):
        return lax.dynamic_slice(weight, (0, target * part, 0), (experts, part, cols))

    def place(held, got, source):
        return lax.dynamic_update_slice(held, got, (0, 0, source * cols))

    return exchange(block, place, count, jnp.zeros((experts, part, cols * count), weight.dtype))


def gather_rows(block):
    return lax.all_gather(block, "shard", axis=0, tiled=True)


def scatter_rows(partial):
    return lax.psum_scatter(partial.astype(BF16), "shard", scatter_dimension=0, tiled=True)


def gelu(value):
    return jax.nn.gelu(value, approximate=True)


def body(
    count,
    tokens,
    cotangent,
    lengths,
    routes,
    buckets,
    w_qkv,
    w_attn_out,
    gains,
    router,
    w_in,
    w_out,
    bias_table,
):
    row_count, width = tokens.shape
    layer_count = w_qkv.shape[0]
    experts = w_in.shape[1]
    slot_count = experts * CAP
    rel_count = buckets.shape[0]

    packed = [w_qkv, w_attn_out[:, None]]
    attn_full = [
        lax.all_gather(
            jnp.concatenate([part[layer] for part in packed], axis=0), "shard", axis=1, tiled=True
        )
        for layer in range(layer_count)
    ]
    small = jnp.concatenate([gains.reshape(-1), router.reshape(-1), bias_table.reshape(-1)])
    small = lax.all_gather(small, "shard", axis=0)
    first, second = gains.size, gains.size + router.size
    own = width // count
    gains_full = (
        small[:, :first]
        .reshape(count, layer_count, 2, own)
        .transpose(1, 2, 0, 3)
        .reshape(layer_count, 2, width)
        .astype(F32)
    )
    router_full = (
        small[:, first:second]
        .reshape(count, layer_count, own, experts)
        .transpose(1, 0, 2, 3)
        .reshape(layer_count, width, experts)
    )
    table_full = small[:, second:].reshape(NB, H).astype(F32)
    inner_full = [columns_from_rows(w_in[layer], count) for layer in range(layer_count)]

    positions = jnp.arange(row_count, dtype=jnp.int32)
    bounds = jnp.cumsum(lengths[0])
    segment = jnp.sum((positions[:, None] >= bounds[None, :]).astype(jnp.int32), axis=1)
    row_seg, col_seg = segment[:, None], segment[None, :]
    live_mask = (positions < bounds[-1]).astype(F32)[:, None]
    bucket_hot = (jnp.arange(NB, dtype=jnp.int32)[:, None] == buckets[None, :]).astype(F32)
    bucket_hot = jnp.pad(bucket_hot, ((0, 0), (0, 2 * row_count - rel_count)))
    rel_pairs = jnp.dot(table_full.T, bucket_hot, precision=HIGHEST).reshape(
        H // 2, 2, 2 * row_count
    )

    def make_plan(layer):
        route = routes[layer, :, 0]
        route_hot = (route[:, None] == jnp.arange(experts, dtype=jnp.int32)[None, :]).astype(
            jnp.int32
        )
        earlier = jnp.cumsum(route_hot, axis=0) - route_hot
        slot_index = route * CAP + jnp.sum(earlier * route_hot, axis=1)
        slots = jnp.arange(slot_count, dtype=jnp.int32)
        placing = (slots[:, None] == slot_index[None, :]).astype(BF16)
        return (placing, route_hot.astype(F32))

    def spread(placing, rows):
        placed = matmul(placing, rows).astype(BF16)
        return [placed[e * CAP : (e + 1) * CAP] for e in range(experts)]

    def collect(placing, parts):
        return matmul(placing, jnp.concatenate(parts, axis=0), ((0,), (0,)))

    hidden = tokens.astype(F32)
    saved = []
    for layer in range(layer_count):
        weights = attn_full[layer]
        placing, route_hot = make_plan(layer)
        scale_one = inverse_rms(hidden)
        normed_one = (hidden * scale_one * gains_full[layer, 0]).astype(BF16)
        qkv = jnp.stack([matmul(normed_one, weights[i]).astype(BF16) for i in range(3)])
        attended = attend_forward(rel_pairs, row_seg, col_seg, qkv)
        middle = hidden + matmul(attended, weights[3])
        scale_two = inverse_rms(middle)
        normed_two = (middle * scale_two * gains_full[layer, 1]).astype(BF16)
        placed = [gather_rows(part) for part in spread(placing, normed_two)]
        logits = matmul(normed_two, router_full[layer])
        shifted = jnp.exp(logits - jnp.max(logits, axis=1, keepdims=True))
        softmax_w = shifted / jnp.sum(shifted, axis=1, keepdims=True)
        gate = jnp.sum(softmax_w * route_hot, axis=1, keepdims=True)
        upward = [matmul(placed[e], inner_full[layer][e]) for e in range(experts)]
        active = [gelu(value).astype(BF16) for value in upward]
        expert_out = [
            scatter_rows(matmul(active[e], w_out[layer, e])) for e in range(experts)
        ]
        combined = collect(placing, expert_out)
        saved.append(
            (
                placing, route_hot, hidden, scale_one, normed_one, qkv, attended, middle,
                scale_two, normed_two, softmax_w, gate, placed, upward, active, combined,
            )
        )
        hidden = middle + gate * combined
    out_tokens = hidden.astype(BF16)

    gradient = cotangent.astype(F32) * live_mask
    attn_grads = [None] * layer_count
    inner_grads = [None] * layer_count
    outer_grads = [None] * layer_count
    gain_grads = [None] * layer_count
    route_grads = [None] * layer_count
    rel_sum = None
    for layer in reversed(range(layer_count)):
        (
            placing, route_hot, hidden, scale_one, normed_one, qkv, attended, middle,
            scale_two, normed_two, softmax_w, gate, placed, upward, active, combined,
        ) = saved[layer]
        weights = attn_full[layer]
        delta_out = [
            gather_rows(part) for part in spread(placing, (gate * gradient).astype(BF16))
        ]
        delta_gate = jnp.sum(gradient * combined, axis=1, keepdims=True)
        delta_logits = (softmax_w * (route_hot - gate) * delta_gate).astype(BF16)
        delta_placed, inner_parts, outer_parts = [], [], []
        for e in range(experts):
            delta_active = matmul(delta_out[e], w_out[layer, e], ((1,), (1,)))
            pull = jax.vjp(gelu, upward[e])[1]
            delta_upward = pull(delta_active)[0].astype(BF16)
            delta_placed.append(
                scatter_rows(matmul(delta_upward, inner_full[layer][e], ((1,), (1,))))
            )
            inner_parts.append(matmul(placed[e], delta_upward, ((0,), (0,))).astype(BF16))
            outer_parts.append(matmul(active[e], delta_out[e], ((0,), (0,))).astype(BF16))
        outer_grads[layer] = lax.psum(jnp.stack(outer_parts), "rep")
        inner_grads[layer] = lax.psum(rows_from_columns(jnp.stack(inner_parts), count), "rep")
        route_grads[layer] = matmul(normed_two, delta_logits, ((0,), (0,)))
        delta_normed_two = collect(placing, delta_placed) + matmul(
            delta_logits, router_full[layer], ((1,), (1,))
        )
        delta_middle, gain_two = norm_backward(
            middle, scale_two, gains_full[layer, 1], delta_normed_two
        )
        delta_middle = delta_middle + gradient
        delta_branch = delta_middle.astype(BF16)
        delta_attended = matmul(delta_branch, weights[3], ((1,), (1,))).astype(BF16)
        delta_qkv, delta_rel = attend_backward(rel_pairs, row_seg, col_seg, qkv, delta_attended)
        rel_sum = delta_rel if rel_sum is None else rel_sum + delta_rel
        projection = [matmul(normed_one, delta_qkv[i], ((0,), (0,))) for i in range(3)]
        projection.append(matmul(attended, delta_branch, ((0,), (0,))))
        attn_part = jnp.stack([part.astype(BF16) for part in projection])
        attn_part = lax.psum_scatter(attn_part, "shard", scatter_dimension=1, tiled=True)
        attn_grads[layer] = lax.psum(attn_part, "rep")
        delta_normed_one = sum(
            matmul(delta_qkv[i], weights[i], ((1,), (1,))) for i in range(3)
        )
        delta_hidden, gain_one = norm_backward(
            hidden, scale_one, gains_full[layer, 0], delta_normed_one
        )
        gradient = delta_hidden + delta_middle
        gain_grads[layer] = jnp.stack([gain_one, gain_two])

    grad_table = jnp.dot(
        bucket_hot, rel_sum.reshape(H, 2 * row_count).T, precision=HIGHEST
    )
    gain_all, route_all = jnp.stack(gain_grads), jnp.stack(route_grads)
    flat = jnp.concatenate([gain_all.reshape(-1), route_all.reshape(-1), grad_table.reshape(-1)])
    flat = lax.psum(flat, ("rep", "shard"))
    first, second = gain_all.size, gain_all.size + route_all.size
    me = lax.axis_index("shard")
    table_rows = NB // count
    grad_gains = lax.dynamic_slice_in_dim(flat[:first].reshape(gain_all.shape), me * own, own, 2)
    grad_router = lax.dynamic_slice_in_dim(
        flat[first:second].reshape(route_all.shape), me * own, own, 1
    )
    grad_table = lax.dynamic_slice_in_dim(
        flat[second:].reshape(NB, H), me * table_rows, table_rows, 0
    )
    attn_all = jnp.stack(attn_grads).astype(F32)
    return (
        out_tokens,
        gradient,
        attn_all[:, :3],
        attn_all[:, 3],
        grad_gains,
        grad_router,
        jnp.stack(inner_grads).astype(F32),
        jnp.stack(outer_grads).astype(F32),
        grad_table,
    )


def solution(mesh):
    rows = P(("rep", "shard"), None)
    weight_specs = (
        P(None, None, "shard", None),
        P(None, "shard", None),
        P(None, None, "shard"),
        P(None, "shard", None),
        P(None, None, "shard", None),
        P(None, None, "shard", None),
        P("shard", None),
    )
    return jax.shard_map(
        functools.partial(body, mesh.shape["shard"]),
        mesh=mesh,
        in_specs=(rows, rows, rows, P(None, ("rep", "shard"), None), P()) + weight_specs,
        out_specs=(rows, rows) + weight_specs,
        check_vma=False,
    )
```

time: 1530 us -> 1170 us (0.76); the launches traced: 1500 us -> 1170 us
  local copies, waits for them, and re-layouts: 697 us -> 70 us
  waiting for transfers between devices: 379 us -> 739 us
  Pallas kernels: 0 us -> 81.2 us
  matrix products: 233 us -> 152 us
  other arithmetic: 103 us -> 37.8 us
    psum x1, waiting for transfers between devices: 0.01 us -> 303 us  [body(): attn_grads[layer] = lax.psum(attn_part, 'rep')]
    unnamed x254 -> x177, local copies, waits for them, and re-layouts: 218 us -> 24.9 us
    rev x2 -> x0, local copies, waits for them, and re-layouts: 190 us -> none  [diagonal_sums(): delta_scores[:, ::-1, :]]
    ppermute x0 -> x12, waiting for transfers between devices: none -> 127 us  [exchange(): got = lax.ppermute(blocks_for(towards), 'shard', pairs)]
    reshape x3 -> x11, local copies, waits for them, and re-layouts: 127 us -> 2.95 us  [the longest x1 1.5 us: body(): route_all.reshape(-1)]
    reduce_scatter x8 -> x10, waiting for transfers between devices: 321 us -> 201 us  [the longest x8 201 us: scatter_rows(): lax.psum_scatter(partial.astype(BF16), 'shard', scatter_dimension=0, tile...]
    slice x12 -> x15, local copies, waits for them, and re-layouts: 101 us -> 13 us  [the longest x4 3.93 us: spread(): return [placed[e * CAP:(e + 1) * CAP] for e in range(experts)]]
    pallas_call x0 -> x4, Pallas kernels: none -> 81.2 us  [the longest x2 45 us: attend_backward(): pl.pallas_call(backward_kernel, grid=(H // 2,), in_specs=attention_specs(...]
  transfers between devices with their start and end apart: 21 -> 33, of which waited for: 6 -> 23; matrix products, arithmetic and copies ran while one was open for 61% -> 16% of each run, Pallas kernels for 0% -> 2%
where the time goes in v1:
time: 1170 us
  waiting for transfers between devices  739 us (63%)
  matrix products  152 us (13%)
  Pallas kernels  81.2 us (7%)
  local copies, waits for them, and re-layouts  70 us (6%)
  blocking collectives  59.4 us (5%)
  other arithmetic  37.8 us (3%)
  between operations  16.8 us (1%)
    psum x1, waiting for transfers between devices, body(): attn_grads[layer] = lax.psum(attn_part, 'rep')  303 us
    reduce_scatter x8, waiting for transfers between devices, scatter_rows(): lax.psum_scatter(partial.astype(BF16), 'shard', scatter_dimension=0, tile...  201 us
    dot_general x62, matrix products, matmul(): return lax.dot_general(a, b, (dims, ((), ())), preferred_element_type=F32)  152 us
    ppermute x12, waiting for transfers between devices, exchange(): got = lax.ppermute(blocks_for(towards), 'shard', pairs)  127 us
    all_gather x2, waiting for transfers between devices, body(): lax.all_gather(jnp.concatenate([part[layer] for part in packed], axis=0),...  55 us
    all_gather x8, waiting for transfers between devices, gather_rows(): return lax.all_gather(block, 'shard', axis=0, tiled=True)  50.3 us
    psum x1, blocking collectives, body(): flat = lax.psum(flat, ('rep', 'shard'))  46.2 us
    pallas_call x2, Pallas kernels, attend_backward(): pl.pallas_call(backward_kernel, grid=(H // 2,), in_specs=attention_specs(...  45 us
  transfers between devices with their start and end apart: 33, of which 23 were waited for; matrix products, arithmetic and copies ran while one was open for 16% of the time, Pallas kernels for 2%

profile of v1, /device:TPU:0, one launch (start us, length us, event | category | flops | bytes accessed | tf_op | source)
XLA Modules:
  0.0 1165.9 jit_solution(11426615725224514868)
XLA Ops:
  16.7 13.2 %all-reduce.1 = bf16[6528]{0:T(1024)(128)(2,1)S(1)} all-reduce(bf16[6528]{0:T(1024)(128)(2,1)S(1)} %dynamic-update-slice), channel_id=2, replica_groups=mesh['rep'=8,'shard'=4] {'shard'}, use_global_device_ids=true, to_apply=%add.1 | all-reduce | flops 6528 | bytes 26112
  32.5 20.6 %all-gather.12.cloned.1.call-done = bf16[4,768,768]{2,1,0:T(8,128)(2,1)} async-done(((bf16[4,192,768]{2,1,0:T(8,128)(2,1)}), bf16[4,768,768]{2,1,0:T(8,128)(2,1)}) %all-gather.12.cloned.1.call-update) | async-done | bytes 4718608 | tf_op jit(solution)/shard_map/all_gather | solution.py:249
  58.7 18.1 %attend_forward.2 = bf16[512,768]{1,0:T(8,128)(2,1)S(1)} custom-call(f32[6,2,1024]{2,1,0:T(2,128)S(1)} %copy.63.rel_ref, s32[512,1]{1,0:T(8,128)S(1)} %copy.64.row_seg_ref, s32[1,512]{1,0:T(1,128)S(1)} %bitcast.314, bf16[3,512,768]{2,1,0:T(8,128)(2,1)S(1)} %pad_maximum_fusion.2.q_ref.k_ref.v_ref, ...), custom_call_target="tpu_custom_call" | custom-call | flops 3221225472 | bytes 3145728 | tf_op jit(solution)/shard_map/attend_forward/pallas_call | solution.py:138
  81.0 4.1 fusion.207
  92.8 19.4 %collective-permute-done = bf16[2,192,768]{2,1,0:T(8,128)(2,1)} collective-permute-done((bf16[2,192,768]{2,1,0:T(8,128)(2,1)}, bf16[2,192,768]{2,1,0:T(8,128)(2,1)}, u32[]{:S(2)}, u32[]{:S(2)}) %collective-permute-start) | collective-permute-done | bytes 589856 | tf_op jit(solution)/shard_map/ppermute | solution.py:183
  116.1 9.9 collective-permute-done.2
  133.2 4.7 convolution_convert_fusion.6
  143.1 4.8 convolution_convert_fusion.7
  155.2 15.7 %reduce-scatter.13.cloned.1.call-done = bf16[288,768]{1,0:T(8,128)(2,1)} async-done(((bf16[1152,768]{1,0:T(8,128)(2,1)}), bf16[288,768]{1,0:T(8,128)(2,1)}) %reduce-scatter.13.cloned.1.call-update) | async-done | bytes 442384 | tf_op jit(solution)/shard_map/reduce_scatter | solution.py:219
  170.8 32.1 %reduce-scatter.11.cloned.1.call-done = bf16[288,768]{1,0:T(8,128)(2,1)} async-done(((bf16[1152,768]{1,0:T(8,128)(2,1)}), bf16[288,768]{1,0:T(8,128)(2,1)}) %reduce-scatter.11.cloned.1.call-update) | async-done | bytes 442384 | tf_op jit(solution)/shard_map/reduce_scatter | solution.py:219
  202.9 3.8 multiply_reduce_fusion.9
  208.0 34.3 %all-gather.18.cloned.1.call-done = bf16[4,768,768]{2,1,0:T(8,128)(2,1)} async-done(((bf16[4,192,768]{2,1,0:T(8,128)(2,1)}), bf16[4,768,768]{2,1,0:T(8,128)(2,1)}) %all-gather.18.cloned.1.call-update) | async-done | bytes 4718608 | tf_op jit(solution)/shard_map/all_gather | solution.py:249
  247.7 18.1 %attend_forward.3 = bf16[512,768]{1,0:T(8,128)(2,1)S(1)} custom-call(f32[6,2,1024]{2,1,0:T(2,128)S(1)} %copy.63.rel_ref, s32[512,1]{1,0:T(8,128)S(1)} %copy.64.row_seg_ref, s32[1,512]{1,0:T(1,128)S(1)} %bitcast.315, bf16[3,512,768]{2,1,0:T(8,128)(2,1)S(1)} %pad_maximum_fusion.3.q_ref.k_ref.v_ref, ...), custom_call_target="tpu_custom_call" | custom-call | flops 3221225472 | bytes 3145728 | tf_op jit(solution)/shard_map/attend_forward/pallas_call | solution.py:138
  284.4 16.4 %collective-permute-done.3 = bf16[2,192,768]{2,1,0:T(8,128)(2,1)S(1)} collective-permute-done((bf16[2,192,768]{2,1,0:T(8,128)(2,1)S(1)}, bf16[2,192,768]{2,1,0:T(8,128)(2,1)S(1)}, u32[]{:S(2)}, u32[]{:S(2)}) %collective-permute-start.3) | collective-permute-done | bytes 589856 | tf_op jit(solution)/shard_map/ppermute | solution.py:183
  302.5 14.5 %collective-permute-done.5 = bf16[2,192,768]{2,1,0:T(8,128)(2,1)S(1)} collective-permute-done((bf16[2,192,768]{2,1,0:T(8,128)(2,1)S(1)}, bf16[2,192,768]{2,1,0:T(8,128)(2,1)S(1)}, u32[]{:S(2)}, u32[]{:S(2)}) %collective-permute-start.5) | collective-permute-done | bytes 589856 | tf_op jit(solution)/shard_map/ppermute | solution.py:183
  323.0 4.7 convolution_convert_fusion.4
  333.0 4.7 convolution_convert_fusion.5
  337.8 9.3 all-gather.26.cloned.1.call-done
  347.0 6.0 fusion.27
  354.3 4.2 convolution_convert_fusion.2
  359.1 10.2 all-gather.24.cloned.1.call-done
  369.2 6.0 fusion.20
  376.5 4.2 convolution_convert_fusion.3
  380.8 20.4 %reduce-scatter.17.cloned.1.call-done = bf16[288,768]{1,0:T(8,128)(2,1)} async-done(((bf16[1152,768]{1,0:T(8,128)(2,1)}), bf16[288,768]{1,0:T(8,128)(2,1)}) %reduce-scatter.17.cloned.1.call-update) | async-done | bytes 442384 | tf_op jit(solution)/shard_map/reduce_scatter | solution.py:219
  401.2 32.0 %reduce-scatter.15.cloned.1.call-done = bf16[288,768]{1,0:T(8,128)(2,1)} async-done(((bf16[1152,768]{1,0:T(8,128)(2,1)}), bf16[288,768]{1,0:T(8,128)(2,1)}) %reduce-scatter.15.cloned.1.call-update) | async-done | bytes 442384 | tf_op jit(solution)/shard_map/reduce_scatter | solution.py:219
  438.3 26.9 %reduce-scatter.21.cloned.1.call-done = bf16[288,768]{1,0:T(8,128)(2,1)} async-done(((bf16[1152,768]{1,0:T(8,128)(2,1)}), bf16[288,768]{1,0:T(8,128)(2,1)}) %reduce-scatter.21.cloned.1.call-update) | async-done | bytes 442384 | tf_op jit(solution)/shard_map/reduce_scatter | solution.py:219
  465.2 32.0 %reduce-scatter.19.cloned.1.call-done = bf16[288,768]{1,0:T(8,128)(2,1)} async-done(((bf16[1152,768]{1,0:T(8,128)(2,1)}), bf16[288,768]{1,0:T(8,128)(2,1)}) %reduce-scatter.19.cloned.1.call-update) | async-done | bytes 442384 | tf_op jit(solution)/shard_map/reduce_scatter | solution.py:219
  497.2 4.1 multiply_reduce_fusion
  506.2 22.5 %attend_backward.2 = (bf16[3,512,768]{2,1,0:T(8,128)(2,1)S(1)}, f32[6,2,1024]{2,1,0:T(2,128)S(1)}) custom-call(f32[6,2,1024]{2,1,0:T(2,128)S(1)} %copy.63.rel_ref, s32[512,1]{1,0:T(8,128)S(1)} %copy.64.row_seg_ref, s32[1,512]{1,0:T(1,128)S(1)} %bitcast.316, bf16[3,512,768]{2,1,0:T(8,128)(2,1)S(1)} %copy-done.1, bf16[3,512,768]{2,1,0:T(8,128)(2,1)S(1)} %copy-done.1, ...), custom_call_target="tpu_custom_call" | custom-call | flops 8053063680 | bytes 6291456 | tf_op jit(solution)/shard_map/attend_backward/pallas_call | solution.py:155
  536.4 20.1 %all-gather.30.cloned.1.call-done = bf16[1152,768]{1,0:T(8,128)(2,1)} async-done(((bf16[288,768]{1,0:T(8,128)(2,1)}), bf16[1152,768]{1,0:T(8,128)(2,1)}) %all-gather.30.cloned.1.call-update) | async-done | bytes 1769488 | tf_op jit(solution)/shard_map/all_gather | solution.py:215
  556.5 6.0 fusion.13
  563.7 4.2 convolution_convert_fusion
  568.0 10.7 all-gather.28.cloned.1.call-done
  578.7 6.0 fusion.6
  586.0 4.2 convolution_convert_fusion.1
  600.4 10.1 reduce-scatter.25.cloned.1.call-done
  610.5 32.0 %reduce-scatter.23.cloned.1.call-done = bf16[288,768]{1,0:T(8,128)(2,1)} async-done(((bf16[1152,768]{1,0:T(8,128)(2,1)}), bf16[288,768]{1,0:T(8,128)(2,1)}) %reduce-scatter.23.cloned.1.call-update) | async-done | bytes 442384 | tf_op jit(solution)/shard_map/reduce_scatter | solution.py:219
  642.5 3.5 multiply_reduce_fusion.2
  649.2 22.5 %attend_backward.3 = (bf16[3,512,768]{2,1,0:T(8,128)(2,1)S(1)}, f32[6,2,1024]{2,1,0:T(2,128)S(1)}) custom-call(f32[6,2,1024]{2,1,0:T(2,128)S(1)} %copy.63.rel_ref, s32[512,1]{1,0:T(8,128)S(1)} %copy.64.row_seg_ref, s32[1,512]{1,0:T(1,128)S(1)} %bitcast.317, bf16[3,512,768]{2,1,0:T(8,128)(2,1)S(1)} %pad_maximum_fusion.2.q_ref.k_ref.v_ref, ...), custom_call_target="tpu_custom_call" | custom-call | flops 8053063680 | bytes 6291456 | tf_op jit(solution)/shard_map/attend_backward/pallas_call | solution.py:155
  692.8 11.9 %collective-permute-done.9 = bf16[2,192,768]{2,1,0:T(8,128)(2,1)S(1)} collective-permute-done((bf16[2,192,768]{2,1,0:T(8,128)(2,1)S(1)}, bf16[2,192,768]{2,1,0:T(8,128)(2,1)S(1)}, u32[]{:S(2)}, u32[]{:S(2)}) %collective-permute-start.9) | collective-permute-done | bytes 589856 | tf_op jit(solution)/shard_map/ppermute | solution.py:183
  704.8 12.6 %collective-permute-done.10 = bf16[2,192,768]{2,1,0:T(8,128)(2,1)S(1)} collective-permute-done((bf16[2,192,768]{2,1,0:T(8,128)(2,1)S(1)}, bf16[2,192,768]{2,1,0:T(8,128)(2,1)S(1)}, u32[]{:S(2)}, u32[]{:S(2)}) %collective-permute-start.10) | collective-permute-done | bytes 589856 | tf_op jit(solution)/shard_map/ppermute | solution.py:183
  730.7 20.4 %collective-permute-done.6 = bf16[2,192,768]{2,1,0:T(8,128)(2,1)S(1)} collective-permute-done((bf16[2,192,768]{2,1,0:T(8,128)(2,1)S(1)}, bf16[2,192,768]{2,1,0:T(8,128)(2,1)S(1)}, u32[]{:S(2)}, u32[]{:S(2)}) %collective-permute-start.6) | collective-permute-done | bytes 589856 | tf_op jit(solution)/shard_map/ppermute | solution.py:183
  751.2 21.4 %collective-permute-done.7 = bf16[2,192,768]{2,1,0:T(8,128)(2,1)S(1)} collective-permute-done((bf16[2,192,768]{2,1,0:T(8,128)(2,1)S(1)}, bf16[2,192,768]{2,1,0:T(8,128)(2,1)S(1)}, u32[]{:S(2)}, u32[]{:S(2)}) %collective-permute-start.7) | collective-permute-done | bytes 589856 | tf_op jit(solution)/shard_map/ppermute | solution.py:183
  784.9 3.5 fusion.36
  788.5 46.2 %psum.51 = f32[6528]{0:T(1024)S(1)} all-reduce(f32[6528]{0:T(1024)S(1)} %pad_maximum_fusion.6), channel_id=1, replica_groups=mesh['rep'=8,'shard'=4] {'rep','shard'}, use_global_device_ids=true, to_apply=%region_40.41 | all-reduce | flops 6528 | bytes 52224 | tf_op jit(solution)/shard_map/psum | solution.py:396
  840.6 303.0 %all-reduce.5.cloned.1.call-done = (bf16[1,4,192,768]{3,2,1,0:T(8,128)(2,1)}, bf16[1,4,192,768]{3,2,1,0:T(8,128)(2,1)}, bf16[1,2,192,3072]{3,2,1,0:T(8,128)(2,1)...) async-done(((bf16[1,4,192,768]{3,2,1,0:T(8,128)(2,1)}, bf16[1,4,192,768]{3,2,1,0:T(8,128)(2,1)}, ...) | async-done | bytes 11796496 | tf_op jit(solution)/shard_map/psum | solution.py:381
  1149.9 4.7 maximum_convert_fusion
  1154.6 4.4 maximum_convert_fusion.1
  (413 shorter events, 184.7 us)
Async XLA Ops:
  7.2 46.0 %all-gather.12.cloned.1.call-start = ((), (), s32[]{:S(2)}) async-start(), calls=%async_computation.10 | async-start | bytes 5898240 | tf_op jit(solution)/shard_map/all_gather | solution.py:249
  11.6 20.1 %copy-start.24 = (bf16[512,768]{1,0:T(8,128)(2,1)S(1)}, bf16[512,768]{1,0:T(8,128)(2,1)}, u32[]{:S(2)}) copy-start(bf16[512,768]{1,0:T(8,128)(2,1)} %param.12) | copy-start | bytes 2359300
  12.7 115.2 %all-gather.16.cloned.1.call-start = ((), (), s32[]{:S(2)}) async-start(), calls=%async_computation.13 | async-start | bytes 2211840 | tf_op jit(solution)/shard_map/all_gather | solution.py:215
  31.7 25.9 %copy-start.43 = (f32[768]{0:T(1024)}, f32[768]{0:T(1024)S(1)}, u32[]{:S(2)}) copy-start(f32[768]{0:T(1024)S(1)} %get-tuple-element.55) | copy-start | bytes 9220
  32.5 25.0 %copy-start.45 = (f32[512]{0:T(512)}, f32[512]{0:T(512)S(1)}, u32[]{:S(2)}) copy-start(f32[512]{0:T(512)S(1)} %get-tuple-element.107) | copy-start | bytes 6148
  78.6 76.2 %copy-start.22 = (bf16[512,768]{1,0:T(8,128)(2,1)}, bf16[512,768]{1,0:T(8,128)(2,1)S(1)}, u32[]{:S(2)}) copy-start(bf16[512,768]{1,0:T(8,128)(2,1)S(1)} %multiply_convert_fusion.8) | copy-start | bytes 2359300
  80.3 57.8 %all-gather.14.cloned.1.call-start = ((), (), s32[]{:S(2)}) async-start(), calls=%async_computation.11 | async-start | bytes 2211840 | tf_op jit(solution)/shard_map/all_gather | solution.py:215
  81.0 89.8 %reduce-scatter.13.cloned.1.call-start = ((), (), s32[]{:S(2)}) async-start(), calls=%async_computation.14 | async-start | bytes 2211840 | tf_op jit(solution)/shard_map/reduce_scatter | solution.py:219
  87.1 25.1 %collective-permute-start = (bf16[2,192,768]{2,1,0:T(8,128)(2,1)}, bf16[2,192,768]{2,1,0:T(8,128)(2,1)}, u32[]{:S(2)}, u32[]{:S(2)}) collective-permute-start(bf16[2,192,768]{2,1,0:T(8,128)(2,1)} %get-tuple-element.83), channel_id=1, source_target_pairs={{0,1},{1,2},{2,3},{3,0},{4,5},{5,6},{6,7},{7,4},{8,9},{9,10},{10,1... | collective-permute-start | bytes 1769480 | tf_op jit(solution)/shard_map/ppermute | solution.py:183
  87.4 26.8 %collective-permute-start.1 = (bf16[2,192,768]{2,1,0:T(8,128)(2,1)}, bf16[2,192,768]{2,1,0:T(8,128)(2,1)}, u32[]{:S(2)}, u32[]{:S(2)}) collective-permute-start(bf16[2,192,768]{2,1,0:T(8,128)(2,1)} %get-tuple-element.82), channel_id=1, source_target_pairs={{0,2},{1,3},{2,0},{3,1},{4,6},{5,7},{6,4},{7,5},{8,10},{9,11},{10,... | collective-permute-start | bytes 1769480 | tf_op jit(solution)/shard_map/ppermute | solution.py:183
  87.7 38.3 %collective-permute-start.2 = (bf16[2,192,768]{2,1,0:T(8,128)(2,1)}, bf16[2,192,768]{2,1,0:T(8,128)(2,1)}, u32[]{:S(2)}, u32[]{:S(2)}) collective-permute-start(bf16[2,192,768]{2,1,0:T(8,128)(2,1)} %get-tuple-element.81), channel_id=1, source_target_pairs={{0,3},{1,0},{2,1},{3,2},{4,7},{5,4},{6,5},{7,6},{8,11},{9,8},{10,9... | collective-permute-start | bytes 1769480 | tf_op jit(solution)/shard_map/ppermute | solution.py:183
  137.9 64.9 %reduce-scatter.11.cloned.1.call-start = ((), (), s32[]{:S(2)}) async-start(), calls=%async_computation.12 | async-start | bytes 2211840 | tf_op jit(solution)/shard_map/reduce_scatter | solution.py:219
  147.9 94.5 %all-gather.18.cloned.1.call-start = ((), (), s32[]{:S(2)}) async-start(), calls=%async_computation.15 | async-start | bytes 5898240 | tf_op jit(solution)/shard_map/all_gather | solution.py:249
  150.5 167.3 %all-gather.22.cloned.1.call-start = ((), (), s32[]{:S(2)}) async-start(), calls=%async_computation.18 | async-start | bytes 2211840 | tf_op jit(solution)/shard_map/all_gather | solution.py:215
  208.0 38.6 %copy-start.38 = (bf16[512,768]{1,0:T(8,128)(2,1)}, bf16[512,768]{1,0:T(8,128)(2,1)S(1)}, u32[]{:S(2)}) copy-start(bf16[512,768]{1,0:T(8,128)(2,1)S(1)} %multiply_convert_fusion.7) | copy-start | bytes 2359300
  269.0 58.9 %all-gather.20.cloned.1.call-start = ((), (), s32[]{:S(2)}) async-start(), calls=%async_computation.16 | async-start | bytes 2211840 | tf_op jit(solution)/shard_map/all_gather | solution.py:215
  269.7 77.3 %all-gather.26.cloned.1.call-start = ((), (), s32[]{:S(2)}) async-start(), calls=%async_computation.22 | async-start | bytes 2211840 | tf_op jit(solution)/shard_map/all_gather | solution.py:215
  276.6 92.6 %all-gather.24.cloned.1.call-start = ((), (), s32[]{:S(2)}) async-start(), calls=%async_computation.20 | async-start | bytes 2211840 | tf_op jit(solution)/shard_map/all_gather | solution.py:215
  277.2 124.0 %reduce-scatter.17.cloned.1.call-start = ((), (), s32[]{:S(2)}) async-start(), calls=%async_computation.19 | async-start | bytes 2211840 | tf_op jit(solution)/shard_map/reduce_scatter | solution.py:219
  278.8 22.0 %collective-permute-start.3 = (bf16[2,192,768]{2,1,0:T(8,128)(2,1)S(1)}, bf16[2,192,768]{2,1,0:T(8,128)(2,1)S(1)}, u32[]{:S(2)}, u32[]{:S(2)}) collective-permute-start(bf16[2,192,768]{2,1,0:T(8,128)(2,1)S(1)} %get-tuple-element.80), channel_id=1, source_target_pairs={{0,1},{1,2},{2,3},{3,0},{4,5},{5,6},{6,7},{7,4},{8,9},{9,10},{10,1... | collective-permute-start | bytes 1769480 | tf_op jit(solution)/shard_map/ppermute | solution.py:183
  279.1 22.5 %collective-permute-start.4 = (bf16[2,192,768]{2,1,0:T(8,128)(2,1)S(1)}, bf16[2,192,768]{2,1,0:T(8,128)(2,1)S(1)}, u32[]{:S(2)}, u32[]{:S(2)}) collective-permute-start(bf16[2,192,768]{2,1,0:T(8,128)(2,1)S(1)} %get-tuple-element.79), channel_id=1, source_target_pairs={{0,2},{1,3},{2,0},{3,1},{4,6},{5,7},{6,4},{7,5},{8,10},{9,11},{10,... | collective-permute-start | bytes 1769480 | tf_op jit(solution)/shard_map/ppermute | solution.py:183
  279.5 37.5 %collective-permute-start.5 = (bf16[2,192,768]{2,1,0:T(8,128)(2,1)S(1)}, bf16[2,192,768]{2,1,0:T(8,128)(2,1)S(1)}, u32[]{:S(2)}, u32[]{:S(2)}) collective-permute-start(bf16[2,192,768]{2,1,0:T(8,128)(2,1)S(1)} %get-tuple-element.78), channel_id=1, source_target_pairs={{0,3},{1,0},{2,1},{3,2},{4,7},{5,4},{6,5},{7,6},{8,11},{9,8},{10,9... | collective-permute-start | bytes 1769480 | tf_op jit(solution)/shard_map/ppermute | solution.py:183
  327.8 105.5 %reduce-scatter.15.cloned.1.call-start = ((), (), s32[]{:S(2)}) async-start(), calls=%async_computation.17 | async-start | bytes 2211840 | tf_op jit(solution)/shard_map/reduce_scatter | solution.py:219
  337.7 127.5 %reduce-scatter.21.cloned.1.call-start = ((), (), s32[]{:S(2)}) async-start(), calls=%async_computation.23 | async-start | bytes 2211840 | tf_op jit(solution)/shard_map/reduce_scatter | solution.py:219
  358.5 138.7 %reduce-scatter.19.cloned.1.call-start = ((), (), s32[]{:S(2)}) async-start(), calls=%async_computation.21 | async-start | bytes 2211840 | tf_op jit(solution)/shard_map/reduce_scatter | solution.py:219
  380.8 175.7 %all-gather.30.cloned.1.call-start = ((), (), s32[]{:S(2)}) async-start(), calls=%async_computation.26 | async-start | bytes 2211840 | tf_op jit(solution)/shard_map/all_gather | solution.py:215
  504.0 28.1 %copy-start.13 = (f32[512,768]{1,0:T(8,128)}, f32[512,768]{1,0:T(8,128)S(1)}, u32[]{:S(2)}) copy-start(f32[512,768]{1,0:T(8,128)S(1)} %get-tuple-element.86) | copy-start | bytes 4718596
  535.6 43.1 %all-gather.28.cloned.1.call-start = ((), (), s32[]{:S(2)}) async-start(), calls=%async_computation.24 | async-start | bytes 2211840 | tf_op jit(solution)/shard_map/all_gather | solution.py:215
  536.1 74.4 %reduce-scatter.25.cloned.1.call-start = ((), (), s32[]{:S(2)}) async-start(), calls=%async_computation.27 | async-start | bytes 2211840 | tf_op jit(solution)/shard_map/reduce_scatter | solution.py:219
  567.9 74.6 %reduce-scatter.23.cloned.1.call-start = ((), (), s32[]{:S(2)}) async-start(), calls=%async_computation.25 | async-start | bytes 2211840 | tf_op jit(solution)/shard_map/reduce_scatter | solution.py:219
  590.2 182.6 %reduce-scatter.29.cloned.1.call-start = ((), (), s32[]{:S(2)}) async-start(), calls=%async_computation.29 | async-start | bytes 5898240 | tf_op jit(solution)/shard_map/reduce_scatter | solution.py:380
  598.2 174.6 %reduce-scatter.27.cloned.1.call-start = ((), (), s32[]{:S(2)}) async-start(), calls=%async_computation.28 | async-start | bytes 5898240 | tf_op jit(solution)/shard_map/reduce_scatter | solution.py:380
  600.4 45.6 %copy-start.48 = (f32[512]{0:T(512)S(1)}, f32[512]{0:T(512)}, u32[]{:S(2)}) copy-start(f32[512]{0:T(512)} %get-tuple-element.108) | copy-start | bytes 6148
  646.5 28.0 %copy-start.11 = (f32[512,768]{1,0:T(8,128)}, f32[512,768]{1,0:T(8,128)S(1)}, u32[]{:S(2)}) copy-start(f32[512,768]{1,0:T(8,128)S(1)} %subtract_add_fusion) | copy-start | bytes 4718596
  649.2 22.5 %copy-start.25 = (bf16[512,768]{1,0:T(8,128)(2,1)S(1)}, bf16[512,768]{1,0:T(8,128)(2,1)}, u32[]{:S(2)}) copy-start(bf16[512,768]{1,0:T(8,128)(2,1)} %param.12) | copy-start | bytes 2359300
  649.2 22.5 %copy-start.44 = (f32[768]{0:T(1024)S(1)}, f32[768]{0:T(1024)}, u32[]{:S(2)}) copy-start(f32[768]{0:T(1024)} %copy-done.43) | copy-start | bytes 9220
  649.2 22.5 %copy-start.46 = (f32[512]{0:T(512)S(1)}, f32[512]{0:T(512)}, u32[]{:S(2)}) copy-start(f32[512]{0:T(512)} %copy-done.45) | copy-start | bytes 6148
  678.1 465.5 %all-reduce.5.cloned.1.call-start = ((), (), s32[]{:S(2)}) async-start(), calls=%async_computation.30 | async-start | bytes 23592960 | tf_op jit(solution)/shard_map/psum | solution.py:381
  684.9 32.5 %collective-permute-start.11 = (bf16[2,192,768]{2,1,0:T(8,128)(2,1)S(1)}, bf16[2,192,768]{2,1,0:T(8,128)(2,1)S(1)}, u32[]{:S(2)}, u32[]{:S(2)}) collective-permute-start(bf16[2,192,768]{2,1,0:T(8,128)(2,1)S(1)} %get-tuple-element.75), channel_id=1, source_target_pairs={{0,3},{1,0},{2,1},{3,2},{4,7},{5,4},{6,5},{7,6},{8,11},{9,8},{10,9... | collective-permute-start | bytes 1769480 | tf_op jit(solution)/shard_map/ppermute | solution.py:183
  684.9 19.8 %collective-permute-start.9 = (bf16[2,192,768]{2,1,0:T(8,128)(2,1)S(1)}, bf16[2,192,768]{2,1,0:T(8,128)(2,1)S(1)}, u32[]{:S(2)}, u32[]{:S(2)}) collective-permute-start(bf16[2,192,768]{2,1,0:T(8,128)(2,1)S(1)} %get-tuple-element.76), channel_id=1, source_target_pairs={{0,1},{1,2},{2,3},{3,0},{4,5},{5,6},{6,7},{7,4},{8,9},{9,10},{10,1... | collective-permute-start | bytes 1769480 | tf_op jit(solution)/shard_map/ppermute | solution.py:183
  685.4 31.9 %collective-permute-start.10 = (bf16[2,192,768]{2,1,0:T(8,128)(2,1)S(1)}, bf16[2,192,768]{2,1,0:T(8,128)(2,1)S(1)}, u32[]{:S(2)}, u32[]{:S(2)}) collective-permute-start(bf16[2,192,768]{2,1,0:T(8,128)(2,1)S(1)} %get-tuple-element.77), channel_id=1, source_target_pairs={{0,2},{1,3},{2,0},{3,1},{4,6},{5,7},{6,4},{7,5},{8,10},{9,11},{10,... | collective-permute-start | bytes 1769480 | tf_op jit(solution)/shard_map/ppermute | solution.py:183
  692.8 24.7 %copy-start.59 = (bf16[1152,768]{1,0:T(8,128)(2,1)S(1)}, bf16[1152,768]{1,0:T(8,128)(2,1)}, u32[]{:S(2)}) copy-start(bf16[1152,768]{1,0:T(8,128)(2,1)} %all-gather.16.cloned.1.call-done) | copy-start | bytes 5308420
  692.8 24.7 %copy-start.81 = (bf16[1152,768]{1,0:T(8,128)(2,1)S(1)}, bf16[1152,768]{1,0:T(8,128)(2,1)}, u32[]{:S(2)}) copy-start(bf16[1152,768]{1,0:T(8,128)(2,1)} %copy-done.80) | copy-start | bytes 5308420
  722.6 50.1 %collective-permute-start.8 = (bf16[2,192,768]{2,1,0:T(8,128)(2,1)S(1)}, bf16[2,192,768]{2,1,0:T(8,128)(2,1)S(1)}, u32[]{:S(2)}, u32[]{:S(2)}) collective-permute-start(bf16[2,192,768]{2,1,0:T(8,128)(2,1)S(1)} %get-tuple-element.72), channel_id=1, source_target_pairs={{0,3},{1,0},{2,1},{3,2},{4,7},{5,4},{6,5},{7,6},{8,11},{9,8},{10,9... | collective-permute-start | bytes 1769480 | tf_op jit(solution)/shard_map/ppermute | solution.py:183
  722.7 28.4 %collective-permute-start.6 = (bf16[2,192,768]{2,1,0:T(8,128)(2,1)S(1)}, bf16[2,192,768]{2,1,0:T(8,128)(2,1)S(1)}, u32[]{:S(2)}, u32[]{:S(2)}) collective-permute-start(bf16[2,192,768]{2,1,0:T(8,128)(2,1)S(1)} %get-tuple-element.73), channel_id=1, source_target_pairs={{0,1},{1,2},{2,3},{3,0},{4,5},{5,6},{6,7},{7,4},{8,9},{9,10},{10,1... | collective-permute-start | bytes 1769480 | tf_op jit(solution)/shard_map/ppermute | solution.py:183
  723.4 49.3 %collective-permute-start.7 = (bf16[2,192,768]{2,1,0:T(8,128)(2,1)S(1)}, bf16[2,192,768]{2,1,0:T(8,128)(2,1)S(1)}, u32[]{:S(2)}, u32[]{:S(2)}) collective-permute-start(bf16[2,192,768]{2,1,0:T(8,128)(2,1)S(1)} %get-tuple-element.74), channel_id=1, source_target_pairs={{0,2},{1,3},{2,0},{3,1},{4,6},{5,7},{6,4},{7,5},{8,10},{9,11},{10,... | collective-permute-start | bytes 1769480 | tf_op jit(solution)/shard_map/ppermute | solution.py:183
  784.9 52.7 %copy-start.47 = (f32[512]{0:T(512)S(1)}, f32[512]{0:T(512)}, u32[]{:S(2)}) copy-start(f32[512]{0:T(512)} %get-tuple-element.106) | copy-start | bytes 6148
  788.4 49.2 %copy-start.12 = (f32[512,768]{1,0:T(8,128)S(1)}, f32[512,768]{1,0:T(8,128)}, u32[]{:S(2)}) copy-start(f32[512,768]{1,0:T(8,128)} %copy-done.11) | copy-start | bytes 4718596
  (71 other events, 239.2 us)
Sparse Core Ops, SparseCore 0:
  12.8 40.2 all-gather.11
  80.4 30.1 all-gather.15
  112.1 23.8 all-gather.13
  138.9 31.8 reduce-scatter.12
  173.4 29.4 reduce-scatter.10
  204.9 37.4 all-gather.17
  269.1 27.3 all-gather.21
  298.6 26.0 all-gather.19
  326.2 20.7 all-gather.25
  348.4 20.7 all-gather.23
  371.8 29.3 reduce-scatter.16
  403.8 29.3 reduce-scatter.14
  435.8 29.3 reduce-scatter.20
  467.8 29.3 reduce-scatter.18
  535.7 20.7 all-gather.29
  557.9 20.7 all-gather.27
  581.1 29.3 reduce-scatter.24
  613.1 29.3 reduce-scatter.22
  645.6 52.1 reduce-scatter.28
  701.0 69.6 reduce-scatter.26
  776.4 367.0 all-reduce.4
